TPU v7x, 768 devices: a whole 4x8x12 slice. The times are simulated.
768 devices in a mesh: node: 32 (over x_lo, y, core), feat: 24 (over x_hi, z).
Axes of the slice: x: 4 (x_hi: 2, x_lo: 2; x = x_hi * 2 + x_lo), y: 8, z: 12, core: 2. Of those that a mesh axis runs over, the one named last changes fastest.
Arguments:
- features: bfloat16 [196608, 192], P(('node', 'feat')), may hold values from -6 to 6
- cotangent: bfloat16 [196608, 192], P(('node', 'feat')), may hold values from -6 to 6
- w_self: bfloat16 [192, 192], replicated, may hold values from -0.4375 to 0.4375
- w_neigh: bfloat16 [192, 192], replicated, may hold values from -0.4375 to 0.4375
- degree: int32 [196608], P(('node', 'feat')), may hold values from 4 to 63
- tile_row: int32 [8192], P('node'), may hold values from 0 to 23
- tile_col: int32 [8192], P('node'), may hold values from 0 to 767
- tile_fill: int32 [8192], P('node'), may hold values from 0 to 64, as said below
Outputs:
- input_grad: bfloat16 [196608, 192], P(('node', 'feat'))
- self_grad: float32 [192, 192], replicated
- neigh_grad: float32 [192, 192], replicated
Inputs may be any that keep to these rules, and one draw needn't show every extreme that they name: `tile_fill`: in each node group's 256 slots the nonzero values come first; a zero slot holds no edge; every group has at least 64 nonzero slots, and some group has all 256.
All inputs are finite; a program needn't handle non-finite values.
Results may differ from a plain program's by a relative error of at most 0.0047.
Values may be sent and summed in bfloat16 or wider, within the bound.
A program may use at most 32 MiB of HBM per device.

v0:
```python
import math

import jax
import jax.numpy as jnp
from jax import lax
from jax.sharding import PartitionSpec as P

TILE = 256


panel_count = 32


def tile_pattern(fill_values, seed_values, tile_size):
    rows_idx = lax.broadcasted_iota(jnp.int32, (1, tile_size, tile_size), 1)
    cols_idx = lax.broadcasted_iota(jnp.int32, (1, tile_size, tile_size), 2)
    residue = (
        13 * rows_idx * rows_idx
        + 7 * rows_idx * cols_idx
        + 197 * cols_idx
        + 31 * seed_values[:, None, None]
    ) % 251
    return (residue < fill_values[:, None, None]).astype(jnp.bfloat16)


def add_panel(running, source, source_tiles, target_tiles, fill_values, seed_values):
    tile_size = source.shape[2]
    blocks = jnp.take(source, source_tiles, axis=1)
    pattern = tile_pattern(fill_values, seed_values, tile_size)
    products = jnp.einsum("cpr,prs->cps", blocks, pattern, preferred_element_type=jnp.float32)
    return running.at[:, target_tiles, :].add(products)


def local(features, cotangent, w_self, w_neigh, degree, tile_row, tile_col, tile_fill):
    tile_size = TILE
    scaled = (cotangent.astype(jnp.float32) / degree[:, None].astype(jnp.float32)).astype(
        jnp.bfloat16
    )
    columns = lax.all_to_all(scaled.T, "feat", split_axis=0, concat_axis=1, tiled=True)
    col_width = columns.shape[0]
    row_block = columns.shape[1]
    own_tiles = row_block // tile_size
    tiled = columns.reshape(col_width, own_tiles, tile_size)
    group_count = lax.axis_size("node")
    my_group = lax.axis_index("node")
    slot_cap = tile_fill.shape[0]
    panel_ids = jnp.arange(panel_count, dtype=jnp.int32)
    seed_base = my_group * slot_cap
    turn_count = slot_cap // panel_count

    def one_turn(turn_index, current):
        chosen = turn_index * panel_count + panel_ids
        return add_panel(
            current,
            tiled,
            tile_row[chosen],
            tile_col[chosen],
            tile_fill[chosen],
            seed_base + chosen,
        )

    empty = jnp.zeros((col_width, group_count * own_tiles, tile_size), jnp.float32)
    partial_sums = lax.fori_loop(0, turn_count, one_turn, empty)
    summed = lax.psum_scatter(partial_sums, "node", scatter_dimension=1, tiled=True)
    gathered_cols = summed.reshape(col_width, row_block).astype(jnp.bfloat16)
    gathered = lax.all_to_all(gathered_cols, "feat", split_axis=1, concat_axis=0, tiled=True).T
    input_grad = (
        jnp.dot(cotangent, w_self.T, preferred_element_type=jnp.float32)
        + jnp.dot(gathered, w_neigh.T, preferred_element_type=jnp.float32)
    ).astype(jnp.bfloat16)
    summed_grads = lax.psum(
        (
            jnp.dot(features.T, cotangent, preferred_element_type=jnp.float32),
            jnp.dot(features.T, gathered, preferred_element_type=jnp.float32),
        ),
        ("node", "feat"),
    )
    node_total = features.shape[0] * group_count * lax.axis_size("feat")
    factor_norm = 1.0 / math.sqrt(node_total)
    return (input_grad, summed_grads[0] * factor_norm, summed_grads[1] * factor_norm)


def solution(mesh):
    return jax.shard_map(
        local,
        mesh=mesh,
        in_specs=(
            P(("node", "feat"), None),
            P(("node", "feat"), None),
            P(),
            P(),
            P(("node", "feat")),
            P("node"),
            P("node"),
            P("node"),
        ),
        out_specs=(P(("node", "feat"), None), P(), P()),
        check_vma=False,
    )
```

profile of v0, /device:TPU:1, one launch (start us, length us, event | category | flops | bytes accessed | tf_op | source)
XLA Modules:
  0.0 764.9 jit_solution(8054717048483450179)
XLA Ops:
  9.5 18.4 %all-to-all-start = ((bf16[24,8,256]{2,1,0:T(8,128)(2,1)}), bf16[24,8,256]{2,1,0:T(8,128)(2,1)S(1)}, u32[]{:S(2)}, u32[]{:S(2)}) async-start(bf16[24,8,256]{2,1,0:T(8,128)(2,1)} %fusion.26), calls=%async_computation | async-start | bytes 196608 | tf_op jit(solution)/shard_map/all_to_all | solution.py:39
  27.9 11.2 %all-to-all-done = bf16[24,8,256]{2,1,0:T(8,128)(2,1)S(1)} async-done(((bf16[24,8,256]{2,1,0:T(8,128)(2,1)}), bf16[24,8,256]{2,1,0:T(8,128)(2,1)S(1)}, u32[]{:S(2)}, u32[]{:S(2)}) %all-to-all-start) | async-done | bytes 98336 | tf_op jit(solution)/shard_map/all_to_all | solution.py:39
  39.1 3.1 broadcast_in_dim.44
  42.2 101.7 %while.16 = (s32[]{:T(128)}, f32[8,768,256]{2,0,1:T(8,128)}, s32[256]{0:T(256)S(1)}, s32[]{:T(128)}, s32[256]{0:T(256)S(1)}, /*index=5*/s32[256]{0:T(256)S(1)}, bf16[8,24,256]{2,0,1:T(8,128)(2,1)S(1)}, s32[]{:T(128)}, s32[]{:T(128)}) while((s32[]{:T(128)}, f32[8,768,256]{2,0,1:T(8,128)}, s32[256]{0:T(256)S(1)}, s32[]{:T(128)}, ...), condition=%wide.region_2.3_spmd.clone, body=%wide.region_0.2_spmd.clone.sunk | while | flops 50663008 | bytes 1983413 | solution.py:63
  44.4 5.7 fusion.50
  50.9 4.0 scatter_fusion
  57.1 5.7 fusion.50
  63.6 4.0 scatter_fusion
  69.8 5.7 fusion.50
  76.3 4.0 scatter_fusion
  82.5 5.7 fusion.50
  89.0 4.0 scatter_fusion
  95.2 5.7 fusion.50
  101.7 4.0 scatter_fusion
  107.9 5.7 fusion.50
  114.4 4.0 scatter_fusion
  120.6 5.7 fusion.50
  127.1 4.0 scatter_fusion
  133.3 5.7 fusion.50
  139.8 4.0 scatter_fusion
  143.9 123.4 %reduce-scatter.2.cloned.1.call-done = f32[8,24,256]{2,0,1:T(8,128)} async-done(((f32[8,768,256]{2,0,1:T(8,128)}), f32[8,24,256]{2,0,1:T(8,128)}) %reduce-scatter.2.cloned.1.call-update) | async-done | bytes 196624 | tf_op jit(solution)/shard_map/reduce_scatter | solution.py:64
  268.9 10.8 %all-to-all-start.1 = ((bf16[8,24,256]{2,0,1:T(8,128)(2,1)}), bf16[8,24,256]{2,0,1:T(8,128)(2,1)S(1)}, u32[]{:S(2)}, u32[]{:S(2)}) async-start(bf16[8,24,256]{2,0,1:T(8,128)(2,1)} %convert_element_type.23), calls=%async_computation.2 | async-start | bytes 196608 | tf_op jit(solution)/shard_map/all_to_all | solution.py:66
  280.7 10.2 %all-to-all-done.1 = bf16[8,24,256]{2,0,1:T(8,128)(2,1)S(1)} async-done(((bf16[8,24,256]{2,0,1:T(8,128)(2,1)}), bf16[8,24,256]{2,0,1:T(8,128)(2,1)S(1)}, u32[]{:S(2)}, u32[]{:S(2)}) %all-to-all-start.1) | async-done | bytes 98336 | tf_op jit(solution)/shard_map/all_to_all | solution.py:66
  292.6 463.7 %all-reduce.3.cloned.1.call-done = (f32[192,192]{1,0:T(8,128)}, f32[192,192]{1,0:T(8,128)}) async-done(((f32[192,192]{1,0:T(8,128)}, f32[192,192]{1,0:T(8,128)}), (f32[192,192]{1,0:T(8,128)}, f32[192,192]{1,0:T(8,128)})) %all-reduce.3.cloned.1.call-update) | async-done | bytes 294928 | tf_op jit(solution)/shard_map/psum | solution.py:71
  (138 shorter events, 31.6 us)
Async XLA Ops:
  7.2 272.5 %copy-start = (bf16[256,192]{0,1:T(8,128)(2,1)S(1)}, bf16[256,192]{0,1:T(8,128)(2,1)}, u32[]{:S(2)}) copy-start(bf16[256,192]{0,1:T(8,128)(2,1)} %param.10) | copy-start | bytes 294916
  7.2 35.0 %copy-start.3 = (s32[256]{0:T(256)S(1)}, s32[256]{0:T(256)}, u32[]{:S(2)}) copy-start(s32[256]{0:T(256)} %param.15) | copy-start | bytes 3076
  7.2 35.0 %copy-start.1 = (s32[256]{0:T(256)S(1)}, s32[256]{0:T(256)}, u32[]{:S(2)}) copy-start(s32[256]{0:T(256)} %param.16) | copy-start | bytes 3076
  7.2 35.0 %copy-start.2 = (s32[256]{0:T(256)S(1)}, s32[256]{0:T(256)}, u32[]{:S(2)}) copy-start(s32[256]{0:T(256)} %param.17) | copy-start | bytes 3076
  9.5 29.6 %all-to-all-start = ((bf16[24,8,256]{2,1,0:T(8,128)(2,1)}), bf16[24,8,256]{2,1,0:T(8,128)(2,1)S(1)}, u32[]{:S(2)}, u32[]{:S(2)}) async-start(bf16[24,8,256]{2,1,0:T(8,128)(2,1)} %fusion.26), calls=%async_computation | async-start | bytes 196608 | tf_op jit(solution)/shard_map/all_to_all | solution.py:39
  27.9 239.4 %reduce-scatter.2.cloned.1.call-start = ((), (), s32[]{:S(2)}) async-start(), calls=%async_computation.3 | async-start | bytes 6488064 | tf_op jit(solution)/shard_map/reduce_scatter | solution.py:64
  143.8 135.9 %copy-start.4 = (bf16[256,192]{0,1:T(8,128)(2,1)S(1)}, bf16[256,192]{0,1:T(8,128)(2,1)}, u32[]{:S(2)}) copy-start(bf16[256,192]{0,1:T(8,128)(2,1)} %param.11) | copy-start | bytes 294916
  143.8 136.7 %copy-start.5 = (bf16[192,192]{1,0:T(8,128)(2,1)S(1)}, bf16[192,192]{1,0:T(8,128)(2,1)}, u32[]{:S(2)}) copy-start(bf16[192,192]{1,0:T(8,128)(2,1)} %param.12) | copy-start | bytes 221188
  143.8 148.0 %copy-start.6 = (bf16[192,192]{1,0:T(8,128)(2,1)S(1)}, bf16[192,192]{1,0:T(8,128)(2,1)}, u32[]{:S(2)}) copy-start(bf16[192,192]{1,0:T(8,128)(2,1)} %param.13) | copy-start | bytes 221188
  268.9 22.0 %all-to-all-start.1 = ((bf16[8,24,256]{2,0,1:T(8,128)(2,1)}), bf16[8,24,256]{2,0,1:T(8,128)(2,1)S(1)}, u32[]{:S(2)}, u32[]{:S(2)}) async-start(bf16[8,24,256]{2,0,1:T(8,128)(2,1)} %convert_element_type.23), calls=%async_computation.2 | async-start | bytes 196608 | tf_op jit(solution)/shard_map/all_to_all | solution.py:66
  279.6 476.7 %all-reduce.3.cloned.1.call-start = ((), (), s32[]{:S(2)}) async-start(), calls=%async_computation.4 | async-start | bytes 786432 | tf_op jit(solution)/shard_map/psum | solution.py:71
Sparse Core Ops, SparseCore 0:
  144.0 123.2 reduce-scatter.1
  291.9 464.3 all-reduce.2
where the time goes:
time: 766 us; the launch traced here: 765 us
  waiting for transfers between devices  608 us (79%)
  matrix products  48.6 us (6%)
  other arithmetic  39.5 us (5%)
  starting transfers between devices  29.2 us (4%)
  local copies, waits for them, and re-layouts  24.7 us (3%)
  between operations  14.1 us (2%)
    psum x1, waiting for transfers between devices, local(): lax.psum((jnp.dot(features.T, cotangent, preferred_element_type=jnp.float...  464 us
    reduce_scatter x1, waiting for transfers between devices, local(): lax.psum_scatter(partial_sums, 'node', scatter_dimension=1, tiled=True)  123 us
    dot_general x8, matrix products, add_panel(): jnp.einsum('cpr,prs->cps', blocks, pattern, preferred_element_type=jnp.fl...  45.9 us
    scatter-add x8, other arithmetic, add_panel(): return running.at[:, target_tiles, :].add(products)  32.3 us
    all_to_all x1, starting transfers between devices, local(): lax.all_to_all(scaled.T, 'feat', split_axis=0, concat_axis=1, tiled=True)  18.4 us
  transfers between devices with their start and end apart: 4, of which 4 were waited for; matrix products, arithmetic and copies ran while one was open for 0% of the time, Pallas kernels for 0%

commit v1 on v0

v1 whole, which is shorter than its diff:
```python
import functools
import math

import jax
import jax.numpy as jnp
from jax import lax
from jax.experimental import pallas as pl
from jax.experimental.pallas import tpu as pltpu
from jax.sharding import PartitionSpec as P

TILE = 256
HALF = TILE // 2
WIDTH = 8
MOD = 251
UNROLL = 4
MESH = pl.DeviceIdType.MESH
F32 = jnp.float32
BF16 = jnp.bfloat16


def node_coords(node_y):
    me = lax.axis_index("node")
    core = lax.rem(me, 2)
    y = lax.rem(lax.div(me, 2), node_y)
    x = lax.div(me, 2 * node_y)
    return x, y, core


def greet(n_node, n_feat):
    me_n, me_f = lax.axis_index("node"), lax.axis_index("feat")
    barrier = pltpu.get_barrier_semaphore()

    def feat_peer(k, _):
        pl.semaphore_signal(
            barrier, inc=1, device_id={"feat": lax.rem(me_f + k, n_feat)}, device_id_type=MESH
        )
        return 0

    def node_peer(k, _):
        pl.semaphore_signal(
            barrier, inc=1, device_id={"node": lax.rem(me_n + k, n_node)}, device_id_type=MESH
        )
        return 0

    lax.fori_loop(1, n_feat, feat_peer, 0)
    lax.fori_loop(1, n_node, node_peer, 0)
    return barrier, n_feat + n_node - 2


def spread(axis, count, src_of, dst, send_sem, recv_sem):
    me = lax.axis_index(axis)

    def one(k, _):
        peer = lax.rem(me + k, count)
        pltpu.make_async_remote_copy(
            src_ref=src_of(peer),
            dst_ref=dst,
            send_sem=send_sem,
            recv_sem=recv_sem,
            device_id={axis: peer},
            device_id_type=MESH,
        ).start()
        return 0

    lax.fori_loop(1, count, one, 0)


def wait_bytes(view, sem):
    pltpu.make_async_copy(view, view, sem).wait()


class GradSum:
    def __init__(self, n_node, n_feat, local, by_feat, chunk, by_node, out, sems):
        self.n_node, self.n_feat = n_node, n_feat
        self.local, self.by_feat, self.chunk, self.by_node, self.out = (
            local, by_feat, chunk, by_node, out,
        )
        self.sems = sems

    def feat_start(self):
        me = lax.axis_index("feat")
        spread("feat", self.n_feat, lambda p: self.local.at[p], self.by_feat.at[me],
               self.sems.at[0], self.sems.at[1])
        self.by_feat[me] = self.local[me]

    def node_start(self):
        wait_bytes(self.by_feat.at[pl.ds(0, self.n_feat - 1)], self.sems.at[1])
        me = lax.axis_index("node")
        total = jnp.sum(self.by_feat[...], axis=0)
        self.chunk[...] = total
        spread("node", self.n_node, lambda p: self.chunk, self.by_node.at[me],
               self.sems.at[2], self.sems.at[3])
        self.by_node[me] = total

    def back_start(self, factor):
        wait_bytes(self.by_node.at[pl.ds(0, self.n_node - 1)], self.sems.at[3])
        me = lax.axis_index("feat")
        self.out[me] = jnp.sum(self.by_node[...], axis=0) * factor
        spread("feat", self.n_feat, lambda p: self.out.at[me], self.out.at[me],
               self.sems.at[4], self.sems.at[5])

    def finish(self):
        wait_bytes(self.out.at[pl.ds(0, self.n_feat - 1)], self.sems.at[5])
        wait_bytes(self.local.at[pl.ds(0, self.n_feat - 1)], self.sems.at[0])
        wait_bytes(self.by_node.at[pl.ds(0, self.n_node - 1)], self.sems.at[2])
        wait_bytes(self.out.at[pl.ds(0, self.n_feat - 1)], self.sems.at[4])


def grad_scratch(n_node, n_feat, width):
    return [
        pltpu.VMEM((n_feat, WIDTH, width), F32),
        pltpu.VMEM((n_feat, WIDTH, width), F32),
        pltpu.VMEM((WIDTH, width), F32),
        pltpu.VMEM((n_node, WIDTH, width), F32),
        pltpu.SemaphoreType.DMA((6,)),
    ]


def slot_table(n_node, n_feat, row, col, fill):
    me = lax.axis_index("node")
    slot = lax.broadcasted_iota(jnp.int32, (1, TILE), 1)
    shift = lax.rem(31 * (me * TILE + slot), MOD)
    low = jnp.where(shift == 0, 0, MOD - shift)
    bound = jnp.where(fill > 0, fill + jnp.where(low + fill > MOD, 256 - MOD, 0), 0)
    group = lax.div(col, n_feat)
    member = col - group * n_feat
    key = (jnp.where(fill > 0, group, n_node) * TILE + slot).astype(F32)
    keys = jnp.broadcast_to(key, (TILE, TILE))
    keys_t = keys.T
    rank = jnp.sum((keys_t < keys).astype(F32), axis=0, keepdims=True)
    place = lax.broadcasted_iota(jnp.int32, (TILE, TILE), 0).astype(F32)
    chosen = (place == rank).astype(F32).astype(BF16)
    line = lax.broadcasted_iota(jnp.int32, (8, TILE), 0)
    which = lax.rem(line, 4)
    payload = jnp.where(
        which == 0, low, jnp.where(which == 1, bound, jnp.where(which == 2, row, member))
    ).astype(F32).astype(BF16)
    ordered = lax.dot_general(
        payload, chosen, (((1,), (1,)), ((), ())), preferred_element_type=F32
    )
    head = jnp.where(line[:, :HALF] < 4, ordered[:, :HALF], ordered[:, HALF:])
    edge = (lax.broadcasted_iota(jnp.int32, (1, HALF), 1) * TILE).astype(F32)
    before = jnp.sum((keys_t[:, :HALF] < edge).astype(F32), axis=0, keepdims=True)
    return jnp.concatenate([head, jnp.broadcast_to(before, (8, HALF))], axis=0).astype(BF16)


def exchange_kernel(
    n_node, n_feat, factor,
    feat_ref, cot_ref, deg_ref, row_ref, col_ref, fill_ref,
    blocks, self_out,
    send, g_local, g_feat, g_chunk, g_node, g_sems, a_sems, ring_sems, end_sems,
):
    node_y = n_node // 4
    span = n_feat + 1
    cut = (span * 11) // 25
    x, y, core = node_coords(node_y)
    me_n, me_f = lax.axis_index("node"), lax.axis_index("feat")
    barrier, expected = greet(n_node, n_feat)

    scaled = cot_ref[...].astype(F32).T / deg_ref[...].astype(F32)
    for j in range(n_feat):
        part = scaled[j * WIDTH:(j + 1) * WIDTH]
        send[j] = jnp.concatenate([part[:, :HALF], part[:, HALF:]], axis=0).astype(BF16)
    home = me_n * span
    blocks[home + me_f] = send[me_f]
    pl.semaphore_wait(barrier, expected)
    spread("feat", n_feat, lambda p: send.at[p], blocks.at[home + me_f], a_sems.at[0], a_sems.at[1])

    blocks[home + n_feat] = slot_table(n_node, n_feat, row_ref[...], col_ref[...], fill_ref[...])
    grads = GradSum(n_node, n_feat, g_local, g_feat, g_chunk, g_node, self_out, g_sems)
    g_local[...] = lax.dot_general(
        feat_ref[...], cot_ref[...], (((0,), (0,)), ((), ())), preferred_element_type=F32
    ).reshape(g_local.shape)
    wait_bytes(send.at[pl.ds(0, n_feat - 1)], a_sems.at[1])

    def node_at(xx, yy, cc):
        return (xx * node_y + yy) * 2 + cc

    def view(side, offset, lo, hi):
        xx = x if side == 0 else 1 - x
        yy = lax.rem(y + offset + node_y, node_y)
        return blocks.at[pl.ds(node_at(xx, yy, core) * span + lo, hi - lo)]

    ids = {}

    def move(name, ref, target):
        number = ids.setdefault(name, len(ids))
        pltpu.make_async_remote_copy(
            src_ref=ref, dst_ref=ref, send_sem=end_sems.at[0], recv_sem=ring_sems.at[number],
            device_id={"node": target}, device_id_type=MESH,
        ).start()
        return number

    sent = [0]

    def to_sibling(ref):
        pltpu.make_async_remote_copy(
            src_ref=ref, dst_ref=ref, send_sem=end_sems.at[1], recv_sem=end_sems.at[2],
            device_id={"node": node_at(x, y, 1 - core)}, device_id_type=MESH,
        ).start()

    half = node_y // 2
    near = [(0, cut, span), (0, 0, cut), (1, 0, cut)]
    room = (span + cut) // 2
    far = {1: [(0, cut, room), (0, 0, cut)], -1: [(0, room, span), (1, 0, cut)]}

    def pieces(step, way):
        return near if step < half else far[way]

    def pass_on(step, way, side, lo, hi):
        if step >= half:
            return
        for s2, lo2, hi2 in pieces(step + 1, way):
            if s2 == side and lo2 >= lo and hi2 <= hi:
                target = node_at(x, lax.rem(y + way + node_y, node_y), core)
                move(("y", way, step + 1, s2, lo2), view(side, -way * step, lo2, hi2), target)
                sent[0] += hi2 - lo2

    partner = node_at(1 - x, y, core)

    def to_partner(name, ref, count):
        move(name, ref, partner)
        sent[0] += count

    pending = []
    for side, lo, hi in near[:2]:
        for way in (1, -1):
            pass_on(0, way, side, lo, hi)
        to_partner(("x", 0, 0, lo), view(0, 0, lo, hi), hi - lo)
    to_sibling(view(0, 0, 0, span))
    grads.feat_start()
    wait_bytes(view(1, 0, 0, cut), ring_sems.at[ids[("x", 0, 0, 0)]])
    for way in (1, -1):
        pass_on(0, way, 1, 0, cut)
    to_sibling(view(1, 0, 0, cut))
    pending.append((("x", 0, 0, cut), 0, cut, span))

    for step in range(1, half + 1):
        fresh = []
        for (right, left) in zip(pieces(step, 1), pieces(step, -1)):
            for way, (side, lo, hi) in ((1, right), (-1, left)):
                ref = view(side, -way * step, lo, hi)
                wait_bytes(ref, ring_sems.at[ids[("y", way, step, side, lo)]])
                pass_on(step, way, side, lo, hi)
                if side == 0 and lo >= cut:
                    name = ("x", way, step, lo)
                    to_partner(name, ref, hi - lo)
                    fresh.append((name, -way * step, lo, hi))
                to_sibling(ref)
        for name, offset, lo, hi in pending:
            ref = view(1, offset, lo, hi)
            wait_bytes(ref, ring_sems.at[ids[name]])
            to_sibling(ref)
        pending = fresh
        if step == 1:
            grads.node_start()
        if step == half - 1:
            grads.back_start(factor)
    for name, offset, lo, hi in pending:
        ref = view(1, offset, lo, hi)
        wait_bytes(ref, ring_sems.at[ids[name]])
        to_sibling(ref)
    grads.finish()
    wait_bytes(send.at[pl.ds(0, n_feat - 1)], a_sems.at[0])
    wait_bytes(blocks.at[pl.ds(0, n_node // 2 * span)], end_sems.at[2])
    wait_bytes(blocks.at[pl.ds(0, n_node // 2 * span)], end_sems.at[1])
    wait_bytes(blocks.at[pl.ds(0, sent[0])], end_sems.at[0])


def slots_kernel(n_node, n_feat, blocks, out, acc, base, packed, before, packed_s, before_s, todo, sems):
    span = n_feat + 1
    me = lax.axis_index("node")

    table = blocks[...].reshape(n_node, span, 16, HALF)[:, n_feat].astype(F32).astype(jnp.int32)
    for k in range(2):
        low = table[:, 4 * k, :]
        bound = table[:, 4 * k + 1, :]
        row = table[:, 4 * k + 2, :]
        member = table[:, 4 * k + 3, :]
        first = lax.broadcasted_iota(jnp.int32, (n_node, HALF), 0) * span
        packed[k] = (first + row) + low * 1024 + bound * (1 << 18) + member * (1 << 25)
    before[...] = table[:, 8, :]
    moves = [
        pltpu.make_async_copy(packed, packed_s, sems.at[0]),
        pltpu.make_async_copy(before, before_s, sems.at[1]),
    ]
    for one in moves:
        one.start()

    r = lax.broadcasted_iota(jnp.int32, (TILE, TILE), 0)
    c = lax.broadcasted_iota(jnp.int32, (TILE, TILE), 1)
    residue = lax.rem(13 * r * r + 7 * r * c + 197 * c, MOD)
    base[...] = (residue * 256 - 32768).astype(jnp.int16)
    acc[...] = jnp.zeros_like(acc)
    for one in moves:
        one.wait()

    def collect_group(g, count):
        start, stop = before_s[g, me], before_s[g, me + 1]

        def put(i, at):
            todo[at] = packed_s[lax.div(i, HALF), g, lax.rem(i, HALF)]
            return at + 1

        return lax.fori_loop(start, stop, put, count)

    count = lax.fori_loop(0, n_node, collect_group, 0)
    for k in range(UNROLL - 1):
        todo[count + k] = 0

    def turn(i, _):
        for k in range(UNROLL):
            entry = todo[i * UNROLL + k]
            place = jnp.bitwise_and(entry, 1023)
            low = jnp.bitwise_and(lax.shift_right_logical(entry, 10), 255)
            bound = jnp.bitwise_and(lax.shift_right_logical(entry, 18), 127)
            member = lax.shift_right_logical(entry, 25)
            pair = blocks[place].astype(F32)
            source = jnp.concatenate([pair[:8], pair[8:]], axis=1).astype(BF16)
            moved = base[...] - jnp.full((TILE, TILE), low * 256, jnp.int32).astype(jnp.int16)
            limit = jnp.full((TILE, TILE), bound * 256 - 32768, jnp.int32).astype(jnp.int16)
            pattern = jnp.where(moved < limit, jnp.ones((), BF16), jnp.zeros((), BF16))
            acc[member] += jnp.dot(source, pattern, preferred_element_type=F32)
        return 0

    lax.fori_loop(0, lax.div(count + UNROLL - 1, UNROLL), turn, 0)
    for m in range(n_feat):
        part = acc[m]
        out[m] = jnp.concatenate([part[:, :HALF], part[:, HALF:]], axis=0).astype(BF16)


def finish_kernel(
    n_node, n_feat, factor,
    slices, feat_ref, cot_ref, w_self, w_neigh,
    grad_out, neigh_out,
    own, landed, g_local, g_feat, g_chunk, g_node, g_sems, a_sems,
):
    me_f = lax.axis_index("feat")
    barrier, expected = greet(n_node, n_feat)
    own[...] = lax.dot_general(
        cot_ref[...], w_self[...], (((1,), (1,)), ((), ())), preferred_element_type=F32
    )
    landed[me_f] = slices[me_f]
    pl.semaphore_wait(barrier, expected)
    spread("feat", n_feat, lambda p: slices.at[p], landed.at[me_f], a_sems.at[0], a_sems.at[1])
    wait_bytes(landed.at[pl.ds(0, n_feat - 1)], a_sems.at[1])
    parts = landed[...].astype(F32)
    gathered_t = jnp.concatenate([parts[:, :8], parts[:, 8:]], axis=2).reshape(n_feat * WIDTH, TILE)
    gathered = gathered_t.T.astype(BF16)
    grads = GradSum(n_node, n_feat, g_local, g_feat, g_chunk, g_node, neigh_out, g_sems)
    g_local[...] = lax.dot_general(
        feat_ref[...], gathered, (((0,), (0,)), ((), ())), preferred_element_type=F32
    ).reshape(g_local.shape)
    grads.feat_start()
    grad_out[...] = (
        own[...]
        + lax.dot_general(
            gathered, w_neigh[...], (((1,), (1,)), ((), ())), preferred_element_type=F32
        )
    ).astype(BF16)
    grads.node_start()
    grads.back_start(factor)
    grads.finish()
    wait_bytes(slices.at[pl.ds(0, n_feat - 1)], a_sems.at[0])


def in_vmem(count):
    return [pl.BlockSpec(memory_space=pltpu.VMEM)] * count


def local(n_node, n_feat, features, cotangent, w_self, w_neigh, degree, tile_row, tile_col, tile_fill):
    width = n_feat * WIDTH
    span = n_feat + 1
    factor = 1.0 / math.sqrt(n_node * n_feat * TILE)
    line = (1, TILE)
    blocks, self_grad = pl.pallas_call(
        functools.partial(exchange_kernel, n_node, n_feat, factor),
        out_shape=(
            jax.ShapeDtypeStruct((n_node * span, 16, HALF), BF16),
            jax.ShapeDtypeStruct((n_feat, WIDTH, width), F32),
        ),
        in_specs=in_vmem(6),
        out_specs=tuple(in_vmem(2)),
        scratch_shapes=[
            pltpu.VMEM((n_feat, 16, HALF), BF16),
            *grad_scratch(n_node, n_feat, width),
            pltpu.SemaphoreType.DMA((2,)),
            pltpu.SemaphoreType.DMA((64,)),
            pltpu.SemaphoreType.DMA((3,)),
        ],
        compiler_params=pltpu.CompilerParams(
            collective_id=0, has_side_effects=True, vmem_limit_bytes=32 << 20
        ),
        name="exchange",
    )(
        features, cotangent, degree.reshape(line), tile_row.reshape(line),
        tile_col.reshape(line), tile_fill.reshape(line),
    )
    slices = pl.pallas_call(
        functools.partial(slots_kernel, n_node, n_feat),
        out_shape=jax.ShapeDtypeStruct((n_feat, 16, HALF), BF16),
        in_specs=in_vmem(1),
        out_specs=in_vmem(1)[0],
        scratch_shapes=[
            pltpu.VMEM((n_feat, WIDTH, TILE), F32),
            pltpu.VMEM((TILE, TILE), jnp.int16),
            pltpu.VMEM((2, n_node, HALF), jnp.int32),
            pltpu.VMEM((n_node, HALF), jnp.int32),
            pltpu.SMEM((2, n_node, HALF), jnp.int32),
            pltpu.SMEM((n_node, HALF), jnp.int32),
            pltpu.SMEM((n_node * TILE + UNROLL,), jnp.int32),
            pltpu.SemaphoreType.DMA((2,)),
        ],
        compiler_params=pltpu.CompilerParams(vmem_limit_bytes=32 << 20),
        name="slots",
    )(blocks)
    input_grad, neigh_grad = pl.pallas_call(
        functools.partial(finish_kernel, n_node, n_feat, factor),
        out_shape=(
            jax.ShapeDtypeStruct((TILE, width), BF16),
            jax.ShapeDtypeStruct((n_feat, WIDTH, width), F32),
        ),
        in_specs=in_vmem(5),
        out_specs=tuple(in_vmem(2)),
        scratch_shapes=[
            pltpu.VMEM((TILE, width), F32),
            pltpu.VMEM((n_feat, 16, HALF), BF16),
            *grad_scratch(n_node, n_feat, width),
            pltpu.SemaphoreType.DMA((2,)),
        ],
        compiler_params=pltpu.CompilerParams(
            collective_id=1, has_side_effects=True, vmem_limit_bytes=32 << 20
        ),
        name="finish",
    )(slices, features, cotangent, w_self, w_neigh)
    return input_grad, self_grad.reshape(width, width), neigh_grad.reshape(width, width)


def solution(mesh):
    n_node, n_feat = mesh.shape["node"], mesh.shape["feat"]
    return jax.shard_map(
        functools.partial(local, n_node, n_feat),
        mesh=mesh,
        in_specs=(
            P(("node", "feat"), None),
            P(("node", "feat"), None),
            P(),
            P(),
            P(("node", "feat")),
            P("node"),
            P("node"),
            P("node"),
        ),
        out_specs=(P(("node", "feat"), None), P(), P()),
        check_vma=False,
    )
```

time: 766 us -> 124 us (0.16)
  waiting for transfers between devices: 608 us -> 0 us
  Pallas kernels: 0 us -> 116 us
  matrix products: 48.6 us -> 0 us
  other arithmetic: 39.5 us -> 0 us
  starting transfers between devices: 29.2 us -> 0 us
  local copies, waits for them, and re-layouts: 24.7 us -> 6.84 us
  between operations: 14.1 us -> 0.71 us
    psum x1 -> x0, waiting for transfers between devices: 464 us -> none  [local(): lax.psum((jnp.dot(features.T, cotangent, preferred_element_type=jnp.float...]
    reduce_scatter x1 -> x0, waiting for transfers between devices: 123 us -> none  [local(): lax.psum_scatter(partial_sums, 'node', scatter_dimension=1, tiled=True)]
    pallas_call x0 -> x3, Pallas kernels: none -> 116 us  [the longest x1 59.2 us: local(): pl.pallas_call(functools.partial(exchange_kernel, n_node, n_feat, factor)...]
    dot_general x12 -> x0, matrix products: 48.6 us -> none  [the longest x8 45.9 us: add_panel(): jnp.einsum('cpr,prs->cps', blocks, pattern, preferred_element_type=jnp.fl...]
    scatter-add x8 -> x0, other arithmetic: 32.3 us -> none  [add_panel(): return running.at[:, target_tiles, :].add(products)]
    all_to_all x2 -> x0, starting transfers between devices: 29.2 us -> none  [the longest x1 18.4 us: local(): lax.all_to_all(scaled.T, 'feat', split_axis=0, concat_axis=1, tiled=True)]
    gather x32 -> x0, local copies, waits for them, and re-layouts: 21.6 us -> none  [the longest x8 5.69 us: one_turn(): tile_col[chosen]]
    all_to_all x2 -> x0, waiting for transfers between devices: 21.4 us -> none  [the longest x1 11.2 us: local(): lax.all_to_all(scaled.T, 'feat', split_axis=0, concat_axis=1, tiled=True)]
  transfers between devices with their start and end apart: 4 -> 0, of which waited for: 4 -> 0; matrix products, arithmetic and copies ran while one was open for 0% -> 0% of each run, Pallas kernels for 0% -> 0%
where the time goes in v1:
time: 124 us
  Pallas kernels  116 us (94%)
  local copies, waits for them, and re-layouts  6.84 us (6%)
    pallas_call x1, Pallas kernels, local(): pl.pallas_call(functools.partial(exchange_kernel, n_node, n_feat, factor)...  59.2 us
    pallas_call x1, Pallas kernels, local(): pl.pallas_call(functools.partial(finish_kernel, n_node, n_feat, factor),...  46.7 us
    pallas_call x1, Pallas kernels, local(): pl.pallas_call(functools.partial(slots_kernel, n_node, n_feat), out_shape...  10.1 us
    unnamed x17, local copies, waits for them, and re-layouts  6.84 us

profile of v1, /device:TPU:1, one launch (start us, length us, event | category | flops | bytes accessed | tf_op | source)
XLA Modules:
  0.0 123.5 jit_solution(1676405319906120712)
XLA Ops:
  0.6 0.0 copy-start.1
  0.6 0.0 copy-start
  0.7 1.0 copy.11.feat_ref
  1.7 1.0 copy.12.cot_ref
  2.7 0.0 copy-start.2
  2.7 0.7 copy-done.2
  3.4 0.0 copy-start.3
  3.4 0.7 copy-done.3
  4.0 0.0 copy-start.4
  4.0 0.7 copy-done.4
  4.7 0.0 copy-start.5
  4.7 0.7 copy-done.5
  5.4 59.2 %exchange.1 = (bf16[800,16,128]{2,1,0:T(8,128)(2,1)S(1)}, f32[24,8,192]{2,1,0:T(8,128)S(1)}) custom-call(bf16[256,192]{1,0:T(8,128)(2,1)S(1)} %copy.11.feat_ref, bf16[256,192]{1,0:T(8,128)(2,1)S(1)} %copy.12.cot_ref, s32[1,256]{1,0:T(1,128)S(1)} %bitcast.8, s32[1,256]{1,0:T(1,128)S(1)} %bitcast.9, s32[1,256]{1,0:T(1,128)S(1)} %bitcast.10, s32[1,256]{1,0:T(1,128)S(1)} %bitcast.11), custom_call_target="tpu_custom_call" | custom-call | tf_op jit(solution)/shard_map/exchange/pallas_call | solution.py:376
  64.6 10.1 %slots.1.slices = bf16[24,16,128]{2,1,0:T(8,128)(2,1)S(1)} custom-call(bf16[800,16,128]{2,1,0:T(8,128)(2,1)S(1)} %get-tuple-element.7.blocks), custom_call_target="tpu_custom_call" | custom-call | tf_op jit(solution)/shard_map/slots/pallas_call | solution.py:399
  74.7 0.0 copy-done.1
  74.8 0.0 copy-done
  74.8 46.7 %finish.1 = (bf16[256,192]{1,0:T(8,128)(2,1)S(1)}, f32[24,8,192]{2,1,0:T(8,128)S(1)}) custom-call(bf16[24,16,128]{2,1,0:T(8,128)(2,1)S(1)} %slots.1.slices, bf16[256,192]{1,0:T(8,128)(2,1)S(1)} %copy.11.feat_ref, bf16[256,192]{1,0:T(8,128)(2,1)S(1)} %copy.12.cot_ref, bf16[192,192]{1,0:T(8,128)(2,1)S(1)} %copy-done, bf16[192,192]{1,0:T(8,128)(2,1)S(1)} %copy-done.1), custom_call_target="tpu_custom_call" | custom-call | tf_op jit(solution)/shard_map/finish/pallas_call | solution.py:417
  121.4 0.7 copy.15
  122.2 0.7 copy.18
  122.9 0.7 copy.19
Async XLA Ops:
  0.6 74.1 %copy-start.1 = (bf16[192,192]{1,0:T(8,128)(2,1)S(1)}, bf16[192,192]{1,0:T(8,128)(2,1)}, u32[]{:S(2)}) copy-start(bf16[192,192]{1,0:T(8,128)(2,1)} %w_neigh.1) | copy-start | bytes 221188
  0.6 74.1 %copy-start = (bf16[192,192]{1,0:T(8,128)(2,1)S(1)}, bf16[192,192]{1,0:T(8,128)(2,1)}, u32[]{:S(2)}) copy-start(bf16[192,192]{1,0:T(8,128)(2,1)} %w_self.1) | copy-start | bytes 221188
  2.7 0.7 copy-start.2
  3.4 0.7 copy-start.3
  4.0 0.7 copy-start.4
  4.7 0.7 copy-start.5

commit v2 on v1

v2 whole, which is shorter than its diff:
```python
import functools
import math

import jax
import jax.numpy as jnp
from jax import lax
from jax.experimental import pallas as pl
from jax.experimental.pallas import tpu as pltpu
from jax.sharding import PartitionSpec as P

TILE = 256
HALF = TILE // 2
WIDTH = 8
MOD = 251
UNROLL = 16
MESH = pl.DeviceIdType.MESH
F32 = jnp.float32
BF16 = jnp.bfloat16


def node_coords(node_y):
    me = lax.axis_index("node")
    core = lax.rem(me, 2)
    y = lax.rem(lax.div(me, 2), node_y)
    x = lax.div(me, 2 * node_y)
    return x, y, core


def wrap(value, size):
    return lax.rem(value + size, size)


def far_step(t, size):
    back = lax.div(t + 1, 2)
    return lax.rem(size // 2 + jnp.where(lax.rem(t, 2) == 1, size - back, back), size)


def each_feat(n_feat, act):
    ring = n_feat // 2
    me = lax.axis_index("feat")
    hi, z = lax.div(me, ring), lax.rem(me, ring)

    def one(t, _):
        zz = lax.rem(z + far_step(t, ring), ring)
        act((1 - hi) * ring + zz)
        act(hi * ring + zz)
        return 0

    lax.fori_loop(0, ring - 1, one, 0)
    act((1 - hi) * ring + z)


def each_node(n_node, act):
    ring = n_node // 4
    x, y, core = node_coords(ring)

    def one(t, _):
        yy = lax.rem(y + far_step(t, ring), ring)
        act(((1 - x) * ring + yy) * 2 + 1 - core)
        act(((1 - x) * ring + yy) * 2 + core)
        act((x * ring + yy) * 2 + 1 - core)
        act((x * ring + yy) * 2 + core)
        return 0

    lax.fori_loop(0, ring - 1, one, 0)
    act(((1 - x) * ring + y) * 2 + 1 - core)
    act(((1 - x) * ring + y) * 2 + core)
    act((x * ring + y) * 2 + 1 - core)


def greet(n_node, n_feat):
    barrier = pltpu.get_barrier_semaphore()
    each_feat(n_feat, lambda p: pl.semaphore_signal(
        barrier, inc=1, device_id={"feat": p}, device_id_type=MESH))
    each_node(n_node, lambda p: pl.semaphore_signal(
        barrier, inc=1, device_id={"node": p}, device_id_type=MESH))
    return barrier, n_feat + n_node - 2


def push(src, dst, send_sem, recv_sem, where):
    pltpu.make_async_remote_copy(
        src_ref=src, dst_ref=dst, send_sem=send_sem, recv_sem=recv_sem,
        device_id=where, device_id_type=MESH,
    ).start()


def spread(axis, count, src_of, dst, send_sem, recv_sem):
    each = each_feat if axis == "feat" else each_node
    each(count, lambda p: push(src_of(p), dst, send_sem, recv_sem, {axis: p}))


def wait_bytes(view, sem):
    pltpu.make_async_copy(view, view, sem).wait()


def to_tile(rows):
    left = rows[:, :HALF]
    if rows.shape[1] < HALF:
        left = jnp.concatenate([rows, jnp.zeros((WIDTH, HALF - rows.shape[1]), F32)], axis=1)
    right = jnp.zeros((WIDTH, HALF), F32)
    if rows.shape[1] > HALF:
        over = rows[:, HALF:]
        right = jnp.concatenate([over, right[:, : 2 * HALF - rows.shape[1]]], axis=1)
    return jnp.concatenate([left, right], axis=0)


def from_tiles(tiles, width):
    tiles = tiles.astype(F32)
    return jnp.concatenate([tiles[:, :WIDTH], tiles[:, WIDTH:]], axis=2).reshape(-1, 2 * HALF)[:, :width]


class Ring:
    def __init__(self, size, view, target, near, far, sems, first, send_sem, landed):
        self.size, self.half, self.view, self.target = size, size // 2, view, target
        self.near, self.far, self.sems, self.ids, self.send_sem = near, far, sems, {}, send_sem
        self.first, self.landed, self.sent = first, landed, 0

    def sem(self, name):
        number = self.ids.setdefault(name, len(self.ids))
        return self.sems.at[self.first + number]

    def pieces(self, step, way):
        return self.near if step < self.half else self.far[way]

    def move(self, name, ref, where, count):
        push(ref, ref, self.send_sem, self.sem(name), where)
        self.sent += count

    def pass_on(self, step, way, side, lo, hi):
        if step >= self.half:
            return
        for s2, lo2, hi2 in self.pieces(step + 1, way):
            if s2 == side and lo2 >= lo and hi2 <= hi:
                self.move((way, step + 1, s2, lo2), self.view(side, -way * step, lo2, hi2),
                          self.target(way), hi2 - lo2)

    def receive(self, step):
        for pair in zip(self.pieces(step, 1), self.pieces(step, -1)):
            for way, (side, lo, hi) in zip((1, -1), pair):
                ref = self.view(side, -way * step, lo, hi)
                wait_bytes(ref, self.sem((way, step, side, lo)))
                self.pass_on(step, way, side, lo, hi)
                self.landed(way, step, side, lo, hi, ref)


def slot_table(n_node, n_feat, row, col, fill):
    me = lax.axis_index("node")
    slot = lax.broadcasted_iota(jnp.int32, (1, TILE), 1)
    shift = lax.rem(31 * (me * TILE + slot), MOD)
    low = jnp.where(shift == 0, 0, MOD - shift)
    bound = jnp.where(fill > 0, fill + jnp.where(low + fill > MOD, 256 - MOD, 0), 0)
    group = lax.div(col, n_feat)
    member = col - group * n_feat
    key = (jnp.where(fill > 0, group, n_node) * TILE + slot).astype(F32)
    keys = jnp.broadcast_to(key, (TILE, TILE))
    keys_t = keys.T
    rank = jnp.sum((keys_t < keys).astype(F32), axis=0, keepdims=True)
    place = lax.broadcasted_iota(jnp.int32, (TILE, TILE), 0).astype(F32)
    chosen = (place == rank).astype(F32).astype(BF16)
    line = lax.broadcasted_iota(jnp.int32, (8, TILE), 0)
    which = lax.rem(line, 4)
    payload = jnp.where(
        which == 0, low, jnp.where(which == 1, bound, jnp.where(which == 2, row, member))
    ).astype(F32).astype(BF16)
    ordered = lax.dot_general(
        payload, chosen, (((1,), (1,)), ((), ())), preferred_element_type=F32
    )
    head = jnp.where(line[:, :HALF] < 4, ordered[:, :HALF], ordered[:, HALF:])
    edge = (lax.broadcasted_iota(jnp.int32, (1, HALF), 1) * TILE).astype(F32)
    before = jnp.sum((keys_t[:, :HALF] < edge).astype(F32), axis=0, keepdims=True)
    return jnp.concatenate([head, jnp.broadcast_to(before, (8, HALF))], axis=0).astype(BF16)


def exchange_kernel(
    n_node, n_feat,
    feat_hbm, cot_hbm, deg_hbm, row_hbm, col_hbm, fill_hbm,
    blocks, feats, self_out,
    cot, ints, send, g_send, g_feat, g_node, g_tile, g_back,
    in_sems, a_sems, g_sems, y_sems, z_sems, end_sems,
):
    node_y, ring_z = n_node // 4, n_feat // 2
    span = n_feat + 1
    cut = (span * 11) // 25
    width = cot.shape[0]
    x, y, core = node_coords(node_y)
    me_n, me_f = lax.axis_index("node"), lax.axis_index("feat")
    hi, z = lax.div(me_f, ring_z), lax.rem(me_f, ring_z)
    loads = [
        pltpu.make_async_copy(src, dst, in_sems.at[k])
        for k, (src, dst) in enumerate((
            (cot_hbm, cot), (deg_hbm, ints.at[0]), (feat_hbm, feats.at[me_f]),
            (row_hbm, ints.at[1]), (col_hbm, ints.at[2]), (fill_hbm, ints.at[3]),
        ))
    ]
    for load in loads:
        load.start()
    barrier, expected = greet(n_node, n_feat)
    loads[0].wait()
    loads[1].wait()
    scaled = cot[...].astype(F32) / ints[0].astype(F32)
    for j in range(n_feat):
        part = scaled[j * WIDTH:(j + 1) * WIDTH]
        send[j] = jnp.concatenate([part[:, :HALF], part[:, HALF:]], axis=0).astype(BF16)
    home = me_n * span
    blocks[home + me_f] = send[me_f]
    for load in loads[2:]:
        load.wait()
    blocks[home + n_feat] = slot_table(n_node, n_feat, ints[1], ints[2], ints[3])
    pl.semaphore_wait(barrier, expected)

    spread("feat", n_feat, lambda p: send.at[p], blocks.at[home + me_f], a_sems.at[0], a_sems.at[1])

    def z_view(side, offset, lo, hi_row):
        hh = hi if side == 0 else 1 - hi
        return feats.at[hh * ring_z + wrap(z + offset, ring_z), pl.ds(lo, hi_row - lo)]

    mid = width // 2
    z_near = [(0, 0, mid), (0, mid, width), (1, 0, mid), (1, mid, width)]
    z_ring = Ring(
        ring_z, z_view, lambda way: {"feat": hi * ring_z + wrap(z + way, ring_z)},
        z_near, {1: z_near[:2], -1: z_near[2:]}, z_sems, 0, end_sems.at[3], lambda *_: None,
    )
    for side, lo, up in z_near[:2]:
        for way in (1, -1):
            z_ring.pass_on(0, way, side, lo, up)
        z_ring.move(("x", lo), z_view(0, 0, lo, up), {"feat": (1 - hi) * ring_z + z}, up - lo)

    local = lax.dot_general(
        feats[me_f], cot[...], (((1,), (1,)), ((), ())), preferred_element_type=F32
    )
    for j in range(n_feat):
        g_send[j] = to_tile(local[j * WIDTH:(j + 1) * WIDTH]).astype(BF16)
    g_feat[me_f] = g_send[me_f]
    spread("feat", n_feat, lambda p: g_send.at[p], g_feat.at[me_f], g_sems.at[0], g_sems.at[1])

    def z_partner():
        for side, lo, up in z_near[2:]:
            wait_bytes(z_view(1, 0, lo, up), z_ring.sem(("x", lo)))
            for way in (1, -1):
                z_ring.pass_on(0, way, 1, lo, up)

    z_partner()
    wait_bytes(send.at[pl.ds(0, n_feat - 1)], a_sems.at[1])

    def node_at(xx, yy, cc):
        return (xx * node_y + yy) * 2 + cc

    def y_view(side, offset, lo, up):
        xx = x if side == 0 else 1 - x
        return blocks.at[pl.ds(node_at(xx, wrap(y + offset, node_y), core) * span + lo, up - lo)]

    def to_sibling(ref):
        push(ref, ref, end_sems.at[1], end_sems.at[2], {"node": node_at(x, y, 1 - core)})

    fresh = []

    def y_landed(way, step, side, lo, up, ref):
        if side == 0 and lo >= cut:
            name = ("x", way, step, lo)
            y_ring.move(name, ref, partner, up - lo)
            fresh.append((name, -way * step, lo, up))
        to_sibling(ref)

    partner = {"node": node_at(1 - x, y, core)}
    room = (span + cut) // 2
    y_near = [(0, cut, span), (0, 0, cut), (1, 0, cut)]
    y_ring = Ring(
        node_y, y_view, lambda way: {"node": node_at(x, wrap(y + way, node_y), core)}, y_near,
        {1: [(0, cut, room), (0, 0, cut)], -1: [(0, room, span), (1, 0, cut)]},
        y_sems, 0, end_sems.at[0], y_landed,
    )

    def from_partner():
        waiting = list(fresh)
        fresh.clear()
        return waiting

    def drain(waiting):
        for name, offset, lo, up in waiting:
            ref = y_view(1, offset, lo, up)
            wait_bytes(ref, y_ring.sem(name))
            to_sibling(ref)

    for side, lo, up in ((0, 0, cut), (0, cut, span)):
        y_ring.move(("x", 0, 0, lo), y_view(0, 0, lo, up), partner, up - lo)
        for way in (1, -1):
            y_ring.pass_on(0, way, side, lo, up)
    to_sibling(y_view(0, 0, 0, span))
    fresh.append((("x", 0, 0, cut), 0, cut, span))

    z_ring.receive(1)
    ref = y_view(1, 0, 0, cut)
    wait_bytes(ref, y_ring.sem(("x", 0, 0, 0)))
    for way in (1, -1):
        y_ring.pass_on(0, way, 1, 0, cut)
    to_sibling(ref)
    wait_bytes(g_feat.at[pl.ds(0, n_feat - 1)], g_sems.at[1])
    g_tile[...] = jnp.sum(g_feat[...].astype(F32), axis=0)
    g_node[me_n] = g_tile[...]
    spread("node", n_node, lambda p: g_tile, g_node.at[me_n], g_sems.at[2], g_sems.at[3])

    waiting = from_partner()
    z_step = 1
    for step in range(1, node_y // 2 + 1):
        y_ring.receive(step)
        drain(waiting)
        waiting = from_partner()
        if z_step < ring_z // 2:
            z_step += 1
            z_ring.receive(z_step)
        if step == 1:
            wait_bytes(g_node.at[pl.ds(0, n_node - 1)], g_sems.at[3])
            g_back[me_f] = jnp.sum(g_node[...], axis=0).astype(BF16)
            spread("feat", n_feat, lambda p: g_back.at[me_f], g_back.at[me_f], g_sems.at[4], g_sems.at[5])
    drain(waiting)
    while z_step < ring_z // 2:
        z_step += 1
        z_ring.receive(z_step)

    wait_bytes(g_back.at[pl.ds(0, n_feat - 1)], g_sems.at[5])
    self_out[...] = from_tiles(g_back[...], width) * (1.0 / math.sqrt(n_node * n_feat * TILE))
    wait_bytes(send.at[pl.ds(0, n_feat - 1)], a_sems.at[0])
    wait_bytes(g_send.at[pl.ds(0, n_feat - 1)], g_sems.at[0])
    wait_bytes(g_node.at[pl.ds(0, n_node - 1)], g_sems.at[2])
    wait_bytes(g_back.at[pl.ds(0, n_feat - 1)], g_sems.at[4])
    wait_bytes(blocks.at[pl.ds(0, n_node // 2 * span)], end_sems.at[2])
    wait_bytes(blocks.at[pl.ds(0, n_node // 2 * span)], end_sems.at[1])
    wait_bytes(blocks.at[pl.ds(0, y_ring.sent)], end_sems.at[0])
    wait_bytes(feats.at[pl.ds(0, z_ring.sent // width)], end_sems.at[3])


def slots_kernel(
    n_node, n_feat, blocks, feats, out, neigh_out,
    acc, base, packed, before, packed_s, before_s, todo, sems,
):
    span = n_feat + 1
    me = lax.axis_index("node")

    table = blocks[...].reshape(n_node, span, 16, HALF)[:, n_feat].astype(F32).astype(jnp.int32)
    for k in range(2):
        low = table[:, 4 * k, :]
        bound = table[:, 4 * k + 1, :]
        row = table[:, 4 * k + 2, :]
        member = table[:, 4 * k + 3, :]
        first = lax.broadcasted_iota(jnp.int32, (n_node, HALF), 0) * span
        packed[k] = (first + row) + low * 1024 + bound * (1 << 18) + member * (1 << 25)
    before[...] = table[:, 8, :]
    moves = [
        pltpu.make_async_copy(packed, packed_s, sems.at[0]),
        pltpu.make_async_copy(before, before_s, sems.at[1]),
    ]
    for one in moves:
        one.start()

    r = lax.broadcasted_iota(jnp.int32, (TILE, TILE), 0)
    c = lax.broadcasted_iota(jnp.int32, (TILE, TILE), 1)
    residue = lax.rem(13 * r * r + 7 * r * c + 197 * c, MOD)
    base[...] = (residue * 256 - 32768).astype(jnp.int16)
    acc[...] = jnp.zeros_like(acc)
    for one in moves:
        one.wait()

    def collect_group(g, count):
        start, stop = before_s[g, me], before_s[g, me + 1]

        def put(i, at):
            todo[at] = packed_s[lax.div(i, HALF), g, lax.rem(i, HALF)]
            return at + 1

        return lax.fori_loop(start, stop, put, count)

    count = lax.fori_loop(0, n_node, collect_group, 0)
    for k in range(UNROLL - 1):
        todo[count + k] = 0

    def turn(i, _):
        sums = []
        for k in range(UNROLL):
            entry = todo[i * UNROLL + k]
            place = jnp.bitwise_and(entry, 1023)
            low = jnp.bitwise_and(lax.shift_right_logical(entry, 10), 255)
            bound = jnp.bitwise_and(lax.shift_right_logical(entry, 18), 127)
            pair = blocks[place].astype(F32)
            source = jnp.concatenate([pair[:8], pair[8:]], axis=1).astype(BF16)
            moved = base[...] - jnp.full((TILE, TILE), low * 256, jnp.int32).astype(jnp.int16)
            limit = jnp.full((TILE, TILE), bound * 256 - 32768, jnp.int32).astype(jnp.int16)
            pattern = jnp.where(moved < limit, jnp.ones((), BF16), jnp.zeros((), BF16))
            sums.append((lax.shift_right_logical(entry, 25),
                         jnp.dot(source, pattern, preferred_element_type=F32)))
        for member, product in sums:
            acc[member] += product
        return 0

    lax.fori_loop(0, lax.div(count + UNROLL - 1, UNROLL), turn, 0)
    total = jnp.zeros((WIDTH, feats.shape[1]), F32)
    for m in range(n_feat):
        part = acc[m]
        out[m] = jnp.concatenate([part[:, :HALF], part[:, HALF:]], axis=0).astype(BF16)
        total += lax.dot_general(
            part.astype(BF16), feats[m], (((1,), (1,)), ((), ())), preferred_element_type=F32
        )
    neigh_out[...] = to_tile(total).astype(BF16)


def finish_kernel(
    n_node, n_feat,
    slices, neigh, cot, w_self, w_neigh,
    grad_out, neigh_out,
    landed, g_node, g_back, g_sems, a_sems,
):
    width = cot.shape[0]
    me_n, me_f = lax.axis_index("node"), lax.axis_index("feat")
    barrier, expected = greet(n_node, n_feat)
    landed[me_f] = slices[me_f]
    g_node[me_n] = neigh[...]
    own = jnp.dot(w_self[...], cot[...], preferred_element_type=F32)
    pl.semaphore_wait(barrier, expected)
    spread("node", n_node, lambda p: neigh, g_node.at[me_n], g_sems.at[0], g_sems.at[1])
    spread("feat", n_feat, lambda p: slices.at[p], landed.at[me_f], a_sems.at[0], a_sems.at[1])
    wait_bytes(g_node.at[pl.ds(0, n_node - 1)], g_sems.at[1])
    g_back[me_f] = jnp.sum(g_node[...].astype(F32), axis=0).astype(BF16)
    spread("feat", n_feat, lambda p: g_back.at[me_f], g_back.at[me_f], g_sems.at[2], g_sems.at[3])
    wait_bytes(landed.at[pl.ds(0, n_feat - 1)], a_sems.at[1])
    gathered = from_tiles(landed[...], TILE).astype(BF16)
    grad_out[...] = (
        own + jnp.dot(w_neigh[...], gathered, preferred_element_type=F32)
    ).astype(BF16)
    wait_bytes(g_back.at[pl.ds(0, n_feat - 1)], g_sems.at[3])
    neigh_out[...] = from_tiles(g_back[...], width).T * (1.0 / math.sqrt(n_node * n_feat * TILE))
    wait_bytes(g_back.at[pl.ds(0, n_feat - 1)], g_sems.at[2])
    wait_bytes(g_node.at[pl.ds(0, n_node - 1)], g_sems.at[0])
    wait_bytes(slices.at[pl.ds(0, n_feat - 1)], a_sems.at[0])


def in_vmem(count):
    return [pl.BlockSpec(memory_space=pltpu.VMEM)] * count


def local(n_node, n_feat, features, cotangent, w_self, w_neigh, degree, tile_row, tile_col, tile_fill):
    width = n_feat * WIDTH
    span = n_feat + 1
    line = (1, TILE)
    tile = (16, HALF)
    shape = jax.ShapeDtypeStruct
    dma = pltpu.SemaphoreType.DMA
    cot_t = cotangent.T
    blocks, feats, self_grad = pl.pallas_call(
        functools.partial(exchange_kernel, n_node, n_feat),
        out_shape=(
            shape((n_node * span, *tile), BF16),
            shape((n_feat, width, TILE), BF16),
            shape((width, width), F32),
        ),
        in_specs=[pl.BlockSpec(memory_space=pltpu.HBM)] * 6,
        out_specs=tuple(in_vmem(3)),
        scratch_shapes=[
            pltpu.VMEM((width, TILE), BF16),
            pltpu.VMEM((4, *line), jnp.int32),
            pltpu.VMEM((n_feat, *tile), BF16),
            pltpu.VMEM((n_feat, *tile), BF16),
            pltpu.VMEM((n_feat, *tile), BF16),
            pltpu.VMEM((n_node, *tile), F32),
            pltpu.VMEM(tile, F32),
            pltpu.VMEM((n_feat, *tile), BF16),
            dma((6,)), dma((2,)), dma((6,)), dma((64,)), dma((64,)), dma((4,)),
        ],
        compiler_params=pltpu.CompilerParams(
            collective_id=0, has_side_effects=True, vmem_limit_bytes=32 << 20
        ),
        name="exchange",
    )(
        features.T, cot_t, degree.reshape(line), tile_row.reshape(line),
        tile_col.reshape(line), tile_fill.reshape(line),
    )
    slices, neigh = pl.pallas_call(
        functools.partial(slots_kernel, n_node, n_feat),
        out_shape=(shape((n_feat, *tile), BF16), shape(tile, BF16)),
        in_specs=in_vmem(2),
        out_specs=tuple(in_vmem(2)),
        scratch_shapes=[
            pltpu.VMEM((n_feat, WIDTH, TILE), F32),
            pltpu.VMEM((TILE, TILE), jnp.int16),
            pltpu.VMEM((2, n_node, HALF), jnp.int32),
            pltpu.VMEM((n_node, HALF), jnp.int32),
            pltpu.SMEM((2, n_node, HALF), jnp.int32),
            pltpu.SMEM((n_node, HALF), jnp.int32),
            pltpu.SMEM((n_node * TILE + UNROLL,), jnp.int32),
            dma((2,)),
        ],
        compiler_params=pltpu.CompilerParams(vmem_limit_bytes=32 << 20),
        name="slots",
    )(blocks, feats)
    input_grad, neigh_grad = pl.pallas_call(
        functools.partial(finish_kernel, n_node, n_feat),
        out_shape=(shape((width, TILE), BF16), shape((width, width), F32)),
        in_specs=in_vmem(5),
        out_specs=tuple(in_vmem(2)),
        scratch_shapes=[
            pltpu.VMEM((n_feat, *tile), BF16),
            pltpu.VMEM((n_node, *tile), BF16),
            pltpu.VMEM((n_feat, *tile), BF16),
            dma((4,)), dma((2,)),
        ],
        compiler_params=pltpu.CompilerParams(
            collective_id=1, has_side_effects=True, vmem_limit_bytes=32 << 20
        ),
        name="finish",
    )(slices, neigh, cot_t, w_self, w_neigh)
    return input_grad.T, self_grad, neigh_grad


def solution(mesh):
    n_node, n_feat = mesh.shape["node"], mesh.shape["feat"]
    return jax.shard_map(
        functools.partial(local, n_node, n_feat),
        mesh=mesh,
        in_specs=(
            P(("node", "feat"), None),
            P(("node", "feat"), None),
            P(),
            P(),
            P(("node", "feat")),
            P("node"),
            P("node"),
            P("node"),
        ),
        out_specs=(P(("node", "feat"), None), P(), P()),
        check_vma=False,
    )
```

time: 124 us -> 97.5 us (0.79)
  Pallas kernels: 116 us -> 90.1 us
    pallas_call x2, Pallas kernels: 106 us -> 81.3 us  [the longest x1 59.8 us: local(): pl.pallas_call(functools.partial(exchange_kernel, n_node, n_feat), out_sh...]
    pallas_call x1, Pallas kernels: 10.1 us -> 8.8 us  [local(): pl.pallas_call(functools.partial(slots_kernel, n_node, n_feat), out_shape...]
    unnamed x17 -> x21, local copies, waits for them, and re-layouts: 6.84 us -> 6.5 us
where the time goes in v2:
time: 97.5 us; the launch traced here: 97.2 us
  Pallas kernels  90.1 us (92%)
  local copies, waits for them, and re-layouts  6.5 us (7%)
    pallas_call x1, Pallas kernels, local(): pl.pallas_call(functools.partial(exchange_kernel, n_node, n_feat), out_sh...  59.8 us
    pallas_call x1, Pallas kernels, local(): pl.pallas_call(functools.partial(finish_kernel, n_node, n_feat), out_shap...  21.4 us
    pallas_call x1, Pallas kernels, local(): pl.pallas_call(functools.partial(slots_kernel, n_node, n_feat), out_shape...  8.8 us
    unnamed x21, local copies, waits for them, and re-layouts  6.5 us

profile of v2, /device:TPU:1, one launch (start us, length us, event | category | flops | bytes accessed | tf_op | source)
XLA Modules:
  0.0 97.2 jit_solution(3596706240661763120)
XLA Ops:
  0.6 0.0 copy-start
  0.6 0.9 copy-done
  1.5 0.0 copy-start.2
  1.5 0.9 copy-done.2
  2.4 0.0 copy-start.5
  2.4 0.7 copy-done.5
  3.1 0.0 copy-start.6
  3.1 0.7 copy-done.6
  3.8 0.0 copy-start.7
  3.8 0.7 copy-done.7
  4.5 0.0 copy-start.8
  4.5 0.7 copy-done.8
  5.1 0.0 copy-start.1
  5.1 0.0 copy-start.3
  5.1 0.0 copy-start.4
  5.1 59.8 %exchange.1 = (bf16[800,16,128]{2,1,0:T(8,128)(2,1)S(1)}, bf16[24,192,256]{2,1,0:T(8,128)(2,1)S(1)}, f32[192,192]{1,0:T(8,128)S(1)}) custom-call(bf16[192,256]{1,0:T(8,128)(2,1)S(1)} %bitcast.9, bf16[192,256]{1,0:T(8,128)(2,1)S(1)} %bitcast.7, s32[1,256]{1,0:T(1,128)S(1)} %bitcast.11, s32[1,256]{1,0:T(1,128)S(1)} %bitcast.12, s32[1,256]{1,0:T(1,128)S(1)} %bitcast.13, ...), custom_call_target="tpu_custom_call" | custom-call | tf_op jit(solution)/shard_map/exchange/pallas_call | solution.py:447
  65.0 8.8 %slots.1 = (bf16[24,16,128]{2,1,0:T(8,128)(2,1)S(1)}, bf16[16,128]{1,0:T(8,128)(2,1)S(1)}) custom-call(bf16[800,16,128]{2,1,0:T(8,128)(2,1)S(1)} %get-tuple-element.10.blocks, bf16[24,192,256]{2,1,0:T(8,128)(2,1)S(1)} %get-tuple-element.11.feats), custom_call_target="tpu_custom_call" | custom-call | tf_op jit(solution)/shard_map/slots/pallas_call | solution.py:475
  73.8 0.0 copy-done.1
  73.8 0.0 copy-done.3
  73.8 0.0 copy-done.4
  73.8 21.4 %finish.1 = (bf16[192,256]{1,0:T(8,128)(2,1)S(1)}, f32[192,192]{1,0:T(8,128)S(1)}) custom-call(bf16[24,16,128]{2,1,0:T(8,128)(2,1)S(1)} %get-tuple-element.12.slices, bf16[16,128]{1,0:T(8,128)(2,1)S(1)} %get-tuple-element.13.neigh, bf16[192,256]{1,0:T(8,128)(2,1)S(1)} %bitcast.8, bf16[192,192]{1,0:T(8,128)(2,1)S(1)} %copy-done.3, bf16[192,192]{1,0:T(8,128)(2,1)S(1)} %copy-done.4), custom_call_target="tpu_custom_call" | custom-call | tf_op jit(solution)/shard_map/finish/pallas_call | solution.py:493
  95.3 0.6 copy.14
  95.9 0.7 copy.15
  96.6 0.7 copy.16
Async XLA Ops:
  0.6 0.9 copy-start
  1.5 0.9 copy-start.2
  2.4 0.7 copy-start.5
  3.1 0.7 copy-start.6
  3.8 0.7 copy-start.7
  4.5 0.7 copy-start.8
  5.1 68.7 %copy-start.1 = (bf16[256,192]{0,1:T(8,128)(2,1)S(1)}, bf16[256,192]{0,1:T(8,128)(2,1)}, u32[]{:S(2)}) copy-start(bf16[256,192]{0,1:T(8,128)(2,1)} %param.9) | copy-start | bytes 294916
  5.1 68.7 %copy-start.3 = (bf16[192,192]{1,0:T(8,128)(2,1)S(1)}, bf16[192,192]{1,0:T(8,128)(2,1)}, u32[]{:S(2)}) copy-start(bf16[192,192]{1,0:T(8,128)(2,1)} %w_self.1) | copy-start | bytes 221188
  5.1 68.7 %copy-start.4 = (bf16[192,192]{1,0:T(8,128)(2,1)S(1)}, bf16[192,192]{1,0:T(8,128)(2,1)}, u32[]{:S(2)}) copy-start(bf16[192,192]{1,0:T(8,128)(2,1)} %w_neigh.1) | copy-start | bytes 221188

commit v3 on v2

--- a/solution.py
+++ b/solution.py
@@ -13,6 +13,7 @@
 WIDTH = 8
 MOD = 251
 UNROLL = 16
+ROOM = 256
 MESH = pl.DeviceIdType.MESH
 F32 = jnp.float32
 BF16 = jnp.bfloat16
@@ -143,7 +144,365 @@
                 self.landed(way, step, side, lo, hi, ref)
 
 
+def ranks(key):
+    keys = jnp.broadcast_to(key, (TILE, TILE))
+    keys_t = keys.T
+    rank = jnp.sum((keys_t < keys).astype(F32), axis=0, keepdims=True)
+    place = lax.broadcasted_iota(jnp.int32, (TILE, TILE), 0).astype(F32)
+    return (place == rank).astype(F32).astype(BF16), keys_t
+
+
+def count_below(keys_t, first):
+    edge = ((lax.broadcasted_iota(jnp.int32, (1, HALF), 1) + first) * TILE).astype(F32)
+    return jnp.sum((keys_t[:, :HALF] < edge).astype(F32), axis=0, keepdims=True)
+
+
 def slot_table(n_node, n_feat, row, col, fill):
+    me = lax.axis_index("node")
+    ring_y = n_node // 8
+    slot = lax.broadcasted_iota(jnp.int32, (1, TILE), 1)
+    shift = lax.rem(31 * (me * TILE + slot), MOD)
+    low = jnp.where(shift == 0, 0, MOD - shift)
+    bound = jnp.where(fill > 0, fill + jnp.where(low + fill > MOD, 256 - MOD, 0), 0)
+    group = lax.div(col, n_feat)
+    far = lax.div(group, 4 * ring_y)
+    in_line = group - far * (4 * ring_y)
+    quad = lax.div(in_line, 4)
+    rest = in_line - quad * 4
+    y_lo = lax.div(rest, 2)
+    core = rest - y_lo * 2
+    side = far * 2 + y_lo
+    member = side * n_feat + col - group * n_feat
+    order = (quad * 2 + core) * 4 + side
+    key = (jnp.where(fill > 0, order, n_node) * TILE + slot).astype(F32)
+    chosen, keys_t = ranks(key)
+    line = lax.broadcasted_iota(jnp.int32, (8, TILE), 0)
+    which = lax.rem(line, 4)
+    payload = jnp.where(
+        which == 0, low, jnp.where(which == 1, bound, jnp.where(which == 2, row, member))
+    ).astype(F32).astype(BF16)
+    ordered = lax.dot_general(
+        payload, chosen, (((1,), (1,)), ((), ())), preferred_element_type=F32
+    )
+    head = jnp.where(line[:, :HALF] < 4, ordered[:, :HALF], ordered[:, HALF:])
+    before = count_below(keys_t, 0)
+    return jnp.concatenate([head, jnp.broadcast_to(before, (8, HALF))], axis=0).astype(BF16)
+
+
+def own_slots(sources, span, mine, members, tables):
+    i_at = lax.broadcasted_iota(jnp.int32, (TILE, TILE), 0).astype(F32)
+    p_at = lax.broadcasted_iota(jnp.int32, (TILE, TILE), 1).astype(F32)
+    apart = i_at - p_at
+    lane = lax.broadcasted_iota(jnp.int32, (1, HALF), 1)
+    line = lax.broadcasted_iota(jnp.int32, (8, TILE), 0)
+    total = jnp.zeros((1, 1), F32)
+    found = jnp.zeros((8, TILE), F32)
+    for s in range(sources):
+        table = tables(s).astype(F32)
+        top, before = table[:8], table[8:9]
+        payload = jnp.concatenate([top, jnp.concatenate([top[4:], top[:4]], axis=0)], axis=1)
+        payload = payload + jnp.where(line == 2, float(s * span), 0.0)
+        begin = jnp.sum(jnp.where(lane == 4 * mine, before, 0.0), axis=1, keepdims=True)
+        end = jnp.sum(jnp.where(lane == 4 * mine + 4, before, 0.0), axis=1, keepdims=True)
+        here = (apart == begin - total) & (i_at >= begin) & (i_at < end)
+        found += jnp.dot(
+            payload.astype(BF16), here.astype(F32).astype(BF16), preferred_element_type=F32
+        )
+        total += end - begin
+    place = lax.broadcasted_iota(jnp.int32, (1, TILE), 1).astype(F32)
+    key = jnp.where(place < total, found[3:4], float(members)) * TILE + place
+    chosen, keys_t = ranks(key)
+    ordered = lax.dot_general(
+        found.astype(BF16), chosen, (((1,), (1,)), ((), ())), preferred_element_type=F32
+    ).astype(jnp.int32)
+    packed = (
+        ordered[0:1] + ordered[1:2] * (1 << 8) + ordered[2:3] * (1 << 16) + ordered[3:4] * (1 << 24)
+    )
+    upto = count_below(keys_t, 1).astype(jnp.int32)
+    upto = jnp.concatenate([upto, upto], axis=1)
+    return jnp.where(line == 0, packed, upto), (total > float(ROOM)).astype(F32)
+
+
+def layer_kernel(
+    n_node, n_feat,
+    feat_hbm, cot_hbm, ints, w_self, w_neigh,
+    grad_out, self_out, neigh_out, flag_out,
+    blocks, feats, feat, cot, send, g_send, g_feat, g_node, g_tile, s_back,
+    base, todo, todo_s, sums, partial, parts, slices, landed, paired, n_send, n_node_sum, n_back,
+    in_sems, a_sems, g_sems, y_sems, z_sems, end_sems, c_sems,
+):
+    ring_y, ring_z = n_node // 8, n_feat // 2
+    sources, span = 2 * ring_y, n_feat + 1
+    width = cot.shape[0]
+    factor = 1.0 / math.sqrt(n_node * n_feat * TILE)
+    x, y, core = node_coords(2 * ring_y)
+    y_hi, y_lo = lax.div(y, 2), lax.rem(y, 2)
+    me_n, me_f = lax.axis_index("node"), lax.axis_index("feat")
+    hi, z = lax.div(me_f, ring_z), lax.rem(me_f, ring_z)
+    mine = x * 2 + y_lo
+    loads = [
+        pltpu.make_async_copy(cot_hbm, cot, in_sems.at[0]),
+        pltpu.make_async_copy(feat_hbm, feat, in_sems.at[1]),
+    ]
+    for load in loads:
+        load.start()
+    barrier, expected = greet(n_node, n_feat)
+    loads[0].wait()
+    scaled = cot[...].astype(F32) / ints[0].astype(F32)
+    for j in range(n_feat):
+        part = scaled[j * WIDTH:(j + 1) * WIDTH]
+        send[j] = jnp.concatenate([part[:, :HALF], part[:, HALF:]], axis=0).astype(BF16)
+    home = (y_hi * 2 + core) * span
+    blocks[home + me_f] = send[me_f]
+    loads[1].wait()
+    wide = width // 2
+    feats[me_f] = feat[pl.ds(pl.multiple_of(hi * wide, 16), wide)]
+    pl.semaphore_wait(barrier, expected)
+
+    spread("feat", n_feat, lambda p: send.at[p], blocks.at[home + me_f], a_sems.at[0], a_sems.at[1])
+
+    def z_view(side, offset, lo, up):
+        hh = hi if side == 0 else 1 - hi
+        return feats.at[hh * ring_z + wrap(z + offset, ring_z), pl.ds(lo, up - lo)]
+
+    z_near = [(0, 0, wide), (1, 0, wide)]
+    z_ring = Ring(
+        ring_z, z_view, lambda way: {"feat": hi * ring_z + wrap(z + way, ring_z)},
+        z_near, {1: z_near[:1], -1: z_near[1:]}, z_sems, 0, end_sems.at[3], lambda *_: None,
+    )
+    x_partner = {"feat": (1 - hi) * ring_z + z}
+    push(feat.at[pl.ds(pl.multiple_of((1 - hi) * wide, 16), wide)], feats.at[me_f],
+         end_sems.at[3], z_ring.sem("x"), x_partner)
+    for way in (1, -1):
+        z_ring.pass_on(0, way, 0, 0, wide)
+
+    blocks[home + n_feat] = slot_table(n_node, n_feat, ints[1], ints[2], ints[3])
+    local = lax.dot_general(
+        feat[...], cot[...], (((1,), (1,)), ((), ())), preferred_element_type=F32
+    )
+    for j in range(n_feat):
+        g_send[j] = to_tile(local[j * WIDTH:(j + 1) * WIDTH]).astype(BF16)
+    g_feat[me_f] = g_send[me_f]
+    spread("feat", n_feat, lambda p: g_send.at[p], g_feat.at[me_f], g_sems.at[0], g_sems.at[1])
+    wait_bytes(z_view(1, 0, 0, wide), z_ring.sem("x"))
+    for way in (1, -1):
+        z_ring.pass_on(0, way, 1, 0, wide)
+    z_step = [0]
+
+    def z_turn():
+        if z_step[0] < ring_z // 2:
+            z_step[0] += 1
+            z_ring.receive(z_step[0])
+
+    wait_bytes(send.at[pl.ds(0, n_feat - 1)], a_sems.at[1])
+
+    def node_at(xx, yy, cc):
+        return (xx * 2 * ring_y + yy) * 2 + cc
+
+    def y_view(side, offset, lo, up):
+        return blocks.at[pl.ds((wrap(y_hi + offset, ring_y) * 2 + core) * span + lo, up - lo)]
+
+    def to_sibling(ref):
+        push(ref, ref, end_sems.at[1], end_sems.at[2], {"node": node_at(x, y, 1 - core)})
+
+    cut = span // 2
+    y_near = [(0, 0, cut), (0, cut, span)]
+    y_ring = Ring(
+        ring_y, y_view,
+        lambda way: {"node": node_at(x, wrap(y_hi + way, ring_y) * 2 + y_lo, core)},
+        y_near, {1: y_near[:1], -1: y_near[1:]}, y_sems, 0, end_sems.at[0],
+        lambda way, step, side, lo, up, ref: to_sibling(ref),
+    )
+    for side, lo, up in y_near:
+        for way in (1, -1):
+            y_ring.pass_on(0, way, side, lo, up)
+    to_sibling(y_view(0, 0, 0, span))
+
+    z_turn()
+    wait_bytes(g_feat.at[pl.ds(0, n_feat - 1)], g_sems.at[1])
+    g_tile[...] = jnp.sum(g_feat[...].astype(F32), axis=0).astype(BF16)
+    g_node[me_n] = g_tile[...]
+    spread("node", n_node, lambda p: g_tile, g_node.at[me_n], g_sems.at[2], g_sems.at[3])
+
+    r = lax.broadcasted_iota(jnp.int32, (TILE, TILE), 0)
+    c = lax.broadcasted_iota(jnp.int32, (TILE, TILE), 1)
+    residue = lax.rem(13 * r * r + 7 * r * c + 197 * c, MOD)
+    base[...] = (residue * 256 - 32768).astype(jnp.int16)
+    own = jnp.dot(w_self[...], cot[...], preferred_element_type=F32)
+
+    for step in range(1, ring_y // 2 + 1):
+        y_ring.receive(step)
+        z_turn()
+    wait_bytes(blocks.at[pl.ds(0, ring_y * span)], end_sems.at[2])
+    listed, over = own_slots(
+        sources, span, y_hi * 2 + core, 4 * n_feat, lambda s: blocks[s * span + n_feat]
+    )
+    todo[...] = listed
+    to_scalars = pltpu.make_async_copy(todo, todo_s, in_sems.at[0])
+    to_scalars.start()
+    wait_bytes(g_node.at[pl.ds(0, n_node - 1)], g_sems.at[3])
+    s_back[me_f] = jnp.sum(g_node[...].astype(F32), axis=0).astype(BF16)
+    spread("feat", n_feat, lambda p: s_back.at[me_f], s_back.at[me_f], g_sems.at[4], g_sems.at[5])
+    to_scalars.wait()
+    z_turn()
+
+    def turn(i, running):
+        products = []
+        for k in range(UNROLL):
+            at = i * UNROLL + k
+            entry = todo_s[0, at]
+            member = lax.shift_right_logical(entry, 24)
+            last = lax.shift_right_logical(todo_s[0, jnp.maximum(at - 1, 0)], 24)
+            low = jnp.bitwise_and(entry, 255)
+            bound = jnp.bitwise_and(lax.shift_right_logical(entry, 8), 255)
+            place = jnp.bitwise_and(lax.shift_right_logical(entry, 16), 255)
+            pair = blocks[jnp.minimum(place, sources * span - 1)].astype(F32)
+            source = jnp.concatenate([pair[:8], pair[8:]], axis=1).astype(BF16)
+            moved = base[...] - jnp.full((TILE, TILE), low * 256, jnp.int32).astype(jnp.int16)
+            limit = jnp.full((TILE, TILE), bound * 256 - 32768, jnp.int32).astype(jnp.int16)
+            pattern = jnp.where(moved < limit, jnp.ones((), BF16), jnp.zeros((), BF16))
+            products.append((at, jnp.where(member == last, 1.0, 0.0),
+                             jnp.dot(source, pattern, preferred_element_type=F32)))
+        for at, keep, product in products:
+            running = running * keep + product
+            sums[at] = running
+        return running
+
+    running = jnp.zeros((WIDTH, TILE), F32)
+    turns = ROOM // UNROLL
+    quarter = turns // 4
+    for part in range(4):
+        running = lax.fori_loop(part * quarter, (part + 1) * quarter, turn, running)
+        if part % 2 == 0:
+            z_turn()
+    for m in range(4 * n_feat):
+        upto = todo_s[1, m]
+        under = todo_s[1, m - 1] if m else 0
+        part = sums[jnp.clip(upto - 1, 0, ROOM - 1)] * jnp.where(upto > under, 1.0, 0.0)
+        partial[m // n_feat, m % n_feat] = jnp.concatenate(
+            [part[:, :HALF], part[:, HALF:]], axis=0
+        ).astype(BF16)
+
+    parts[mine] = partial[mine]
+    for dx, dy in ((1, 1), (0, 1), (1, 0)):
+        xx, yy = wrap(x + dx, 2), wrap(y_lo + dy, 2)
+        push(partial.at[xx * 2 + yy], parts.at[mine], c_sems.at[0], c_sems.at[1],
+             {"node": node_at(xx, y_hi * 2 + yy, core)})
+    while z_step[0] < ring_z // 2:
+        z_turn()
+    wait_bytes(parts.at[pl.ds(0, 3)], c_sems.at[1])
+    total = parts[0].astype(F32)
+    for k in range(1, 4):
+        total += parts[k].astype(F32)
+    slices[...] = total.astype(BF16)
+    push(slices, paired, c_sems.at[8], c_sems.at[9], x_partner)
+    landed[me_f] = slices[me_f]
+    wait_bytes(paired, c_sems.at[9])
+    grad = jnp.zeros((2 * WIDTH, wide), F32)
+    for m in range(n_feat):
+        rows = []
+        for ref in (slices, paired):
+            part = ref[m].astype(F32)
+            rows.append(jnp.concatenate([part[:WIDTH], part[WIDTH:]], axis=1))
+        grad += lax.dot_general(
+            jnp.concatenate(rows, axis=0).astype(BF16), feats[m],
+            (((1,), (1,)), ((), ())), preferred_element_type=F32,
+        )
+    swapped = jnp.concatenate([grad[WIDTH:], grad[:WIDTH]], axis=0)
+    grad = jnp.where(hi == 0, grad, swapped)
+    n_send[...] = jnp.concatenate(
+        [grad, jnp.broadcast_to(over, (2 * WIDTH, HALF - wide))], axis=1
+    ).astype(BF16)
+    n_node_sum[me_n] = n_send[...]
+    spread("node", n_node, lambda p: n_send, n_node_sum.at[me_n], c_sems.at[2], c_sems.at[3])
+    spread("feat", n_feat, lambda p: slices.at[p], landed.at[me_f], c_sems.at[4], c_sems.at[5])
+    wait_bytes(s_back.at[pl.ds(0, n_feat - 1)], g_sems.at[5])
+    self_out[...] = from_tiles(s_back[...], width) * factor
+    wait_bytes(n_node_sum.at[pl.ds(0, n_node - 1)], c_sems.at[3])
+    n_back[me_f] = jnp.sum(n_node_sum[...].astype(F32), axis=0).astype(BF16)
+    spread("feat", n_feat, lambda p: n_back.at[me_f], n_back.at[me_f], c_sems.at[6], c_sems.at[7])
+    wait_bytes(landed.at[pl.ds(0, n_feat - 1)], c_sems.at[5])
+    gathered = from_tiles(landed[...], TILE).astype(BF16)
+    grad_out[...] = (
+        own + jnp.dot(w_neigh[...], gathered, preferred_element_type=F32)
+    ).astype(BF16)
+    wait_bytes(send.at[pl.ds(0, n_feat - 1)], a_sems.at[0])
+    wait_bytes(g_send.at[pl.ds(0, n_feat - 1)], g_sems.at[0])
+    wait_bytes(g_node.at[pl.ds(0, n_node - 1)], g_sems.at[2])
+    wait_bytes(s_back.at[pl.ds(0, n_feat - 1)], g_sems.at[4])
+    wait_bytes(blocks.at[pl.ds(0, ring_y * span)], end_sems.at[1])
+    wait_bytes(blocks.at[pl.ds(0, y_ring.sent)], end_sems.at[0])
+    wait_bytes(feats.at[pl.ds(0, z_ring.sent // wide + 1)], end_sems.at[3])
+    wait_bytes(parts.at[pl.ds(0, 3)], c_sems.at[0])
+    wait_bytes(n_node_sum.at[pl.ds(0, n_node - 1)], c_sems.at[2])
+    wait_bytes(landed.at[pl.ds(0, n_feat - 1)], c_sems.at[4])
+    wait_bytes(n_back.at[pl.ds(0, n_feat - 1)], c_sems.at[7])
+    wait_bytes(paired, c_sems.at[8])
+    back = n_back[...].astype(F32)
+    lines = []
+    for half in range(2):
+        part = back[:, half * WIDTH:(half + 1) * WIDTH, :wide].reshape(2, ring_z * WIDTH, wide)
+        lines.append(jnp.concatenate([part[0], part[1]], axis=1))
+    neigh_out[...] = jnp.concatenate(lines, axis=0).T * factor
+    flag_out[...] = jnp.max(back, axis=0)[:, wide:]
+    wait_bytes(n_back.at[pl.ds(0, n_feat - 1)], c_sems.at[6])
+
+
+def in_vmem(count):
+    return [pl.BlockSpec(memory_space=pltpu.VMEM)] * count
+
+
+def few_slots(n_node, n_feat, features, cotangent, w_self, w_neigh, degree, tile_row, tile_col, tile_fill):
+    width = n_feat * WIDTH
+    span = n_feat + 1
+    ring_y = n_node // 8
+    tile = (16, HALF)
+    shape = jax.ShapeDtypeStruct
+    dma = pltpu.SemaphoreType.DMA
+    vmem = pltpu.VMEM
+    ints = jnp.stack([degree, tile_row, tile_col, tile_fill]).reshape(4, 1, TILE)
+    input_grad, self_grad, neigh_grad, flag = pl.pallas_call(
+        functools.partial(layer_kernel, n_node, n_feat),
+        out_shape=(
+            shape((width, TILE), BF16), shape((width, width), F32), shape((width, width), F32),
+            shape((2 * WIDTH, HALF - width // 2), F32),
+        ),
+        in_specs=[pl.BlockSpec(memory_space=pltpu.HBM)] * 2 + in_vmem(3),
+        out_specs=tuple(in_vmem(4)),
+        scratch_shapes=[
+            vmem((2 * ring_y * span, *tile), BF16),
+            vmem((n_feat, width // 2, TILE), BF16),
+            vmem((width, TILE), BF16),
+            vmem((width, TILE), BF16),
+            vmem((n_feat, *tile), BF16),
+            vmem((n_feat, *tile), BF16),
+            vmem((n_feat, *tile), BF16),
+            vmem((n_node, *tile), BF16),
+            vmem(tile, BF16),
+            vmem((n_feat, *tile), BF16),
+            vmem((TILE, TILE), jnp.int16),
+            vmem((8, TILE), jnp.int32),
+            pltpu.SMEM((8, TILE), jnp.int32),
+            vmem((ROOM, WIDTH, TILE), F32),
+            vmem((4, n_feat, *tile), BF16),
+            vmem((4, n_feat, *tile), BF16),
+            vmem((n_feat, *tile), BF16),
+            vmem((n_feat, *tile), BF16),
+            vmem((n_feat, *tile), BF16),
+            vmem(tile, BF16),
+            vmem((n_node, *tile), BF16),
+            vmem((n_feat, *tile), BF16),
+            dma((2,)), dma((2,)), dma((6,)), dma((16,)), dma((64,)), dma((4,)), dma((10,)),
+        ],
+        compiler_params=pltpu.CompilerParams(
+            collective_id=0, has_side_effects=True, vmem_limit_bytes=40 << 20
+        ),
+        name="layer",
+    )(features.T, cotangent.T, ints, w_self, w_neigh)
+    return (input_grad.T, self_grad, neigh_grad), flag[0, 0]
+
+
+def group_table(n_node, n_feat, row, col, fill):
     me = lax.axis_index("node")
     slot = lax.broadcasted_iota(jnp.int32, (1, TILE), 1)
     shift = lax.rem(31 * (me * TILE + slot), MOD)
@@ -205,7 +564,7 @@
     blocks[home + me_f] = send[me_f]
     for load in loads[2:]:
         load.wait()
-    blocks[home + n_feat] = slot_table(n_node, n_feat, ints[1], ints[2], ints[3])
+    blocks[home + n_feat] = group_table(n_node, n_feat, ints[1], ints[2], ints[3])
     pl.semaphore_wait(barrier, expected)
 
     spread("feat", n_feat, lambda p: send.at[p], blocks.at[home + me_f], a_sems.at[0], a_sems.at[1])
@@ -432,11 +791,7 @@
     wait_bytes(slices.at[pl.ds(0, n_feat - 1)], a_sems.at[0])
 
 
-def in_vmem(count):
-    return [pl.BlockSpec(memory_space=pltpu.VMEM)] * count
-
-
-def local(n_node, n_feat, features, cotangent, w_self, w_neigh, degree, tile_row, tile_col, tile_fill):
+def any_slots(n_node, n_feat, features, cotangent, w_self, w_neigh, degree, tile_row, tile_col, tile_fill):
     width = n_feat * WIDTH
     span = n_feat + 1
     line = (1, TILE)
@@ -465,7 +820,7 @@
             dma((6,)), dma((2,)), dma((6,)), dma((64,)), dma((64,)), dma((4,)),
         ],
         compiler_params=pltpu.CompilerParams(
-            collective_id=0, has_side_effects=True, vmem_limit_bytes=32 << 20
+            collective_id=1, has_side_effects=True, vmem_limit_bytes=32 << 20
         ),
         name="exchange",
     )(
@@ -502,11 +857,16 @@
             dma((4,)), dma((2,)),
         ],
         compiler_params=pltpu.CompilerParams(
-            collective_id=1, has_side_effects=True, vmem_limit_bytes=32 << 20
+            collective_id=2, has_side_effects=True, vmem_limit_bytes=32 << 20
         ),
         name="finish",
     )(slices, neigh, cot_t, w_self, w_neigh)
     return input_grad.T, self_grad, neigh_grad
+
+
+def local(n_node, n_feat, *args):
+    done, flag = few_slots(n_node, n_feat, *args)
+    return lax.cond(flag > 0.0, lambda done, args: any_slots(n_node, n_feat, *args), lambda done, args: done, done, args)
 
 
 def solution(mesh):

time: 97.5 us -> 84.2 us (0.86)
  Pallas kernels: 90.1 us -> 79.5 us
  local copies, waits for them, and re-layouts: 6.5 us -> 2.51 us
    pallas_call x3 -> x1, Pallas kernels: 90.1 us -> 79.5 us  [few_slots(): pl.pallas_call(functools.partial(layer_kernel, n_node, n_feat), out_shape...]
    unnamed x21 -> x3, local copies, waits for them, and re-layouts: 6.5 us -> 2 us
where the time goes in v3:
time: 84.2 us; the launch traced here: 84.1 us
  Pallas kernels  79.5 us (94%)
  local copies, waits for them, and re-layouts  2.51 us (3%)
  between operations  1.31 us (2%)
    pallas_call x1, Pallas kernels, few_slots(): pl.pallas_call(functools.partial(layer_kernel, n_node, n_feat), out_shape...  79.5 us
    unnamed x3, local copies, waits for them, and re-layouts  2 us

profile of v3, /device:TPU:1, one launch (start us, length us, event | category | flops | bytes accessed | tf_op | source)
XLA Modules:
  0.0 84.1 jit_solution(7986292090705688810)
XLA Ops:
  0.6 0.7 pad_add_fusion
  1.4 79.5 %layer.1 = (bf16[192,256]{1,0:T(8,128)(2,1)S(1)}, f32[192,192]{1,0:T(8,128)S(1)}, f32[192,192]{1,0:T(8,128)S(1)}, f32[16,32]{1,0:T(8,128)S(1)}) custom-call(bf16[192,256]{1,0:T(8,128)(2,1)} %bitcast.18, bf16[192,256]{1,0:T(8,128)(2,1)} %bitcast.15, s32[4,1,256]{2,1,0:T(1,128)S(1)} %reshape.25.ints, bf16[192,192]{1,0:T(8,128)(2,1)} %w_self.1, ...), custom_call_target="tpu_custom_call" | custom-call | tf_op jit(solution)/shard_map/layer/pallas_call | solution.py:464
  80.9 0.5 slice.3
  82.1 0.6 copy.26
  82.7 0.7 copy.27
  83.4 0.7 copy.28
  (2 shorter events, 0.0 us)
